TPU v7x, 256 devices: a whole 4x4x8 slice. The times are simulated.
256 devices in a mesh: grp: 2 (over core), ctx: 64 (over x, z_lo, y), hd: 2 (over z_hi).
Axes of the slice: x: 4, y: 4, z: 8 (z_hi: 2, z_lo: 4; z = z_hi * 4 + z_lo), core: 2. Of those that a mesh axis runs over, the one named last changes fastest.
Arguments:
- video_q: bfloat16 [8192, 24, 128], P(('ctx', 'hd'), 'grp'), may hold values from -6 to 6
- video_k: bfloat16 [8192, 24, 128], P(('ctx', 'hd'), 'grp'), may hold values from -6 to 6
- video_v: bfloat16 [8192, 24, 128], P(('ctx', 'hd'), 'grp'), may hold values from -6 to 6
- positions: int32 [3, 8192], P(None, ('ctx', 'hd')), may hold values from 0 to 31, as said below
- text_q: bfloat16 [256, 24, 128], P(None, ('grp', 'hd')), may hold values from -16 to 16
- text_k: bfloat16 [256, 24, 128], P(None, ('grp', 'hd')), may hold values from -16 to 16
- text_v: bfloat16 [256, 24, 128], P(None, ('grp', 'hd')), may hold values from -6 to 6
- text_count: int32 [1], replicated, may hold values from 64 to 256
Outputs:
- video_out: bfloat16 [8192, 24, 128], P(('ctx', 'hd'), 'grp')
- text_out: bfloat16 [256, 24, 128], P('ctx', ('grp', 'hd'))
Inputs may be any that keep to these rules, and one draw needn't show every extreme that they name: `positions`: column n holds the frame, row and column of video token n; the columns are distinct cells of a grid of 32 frames of 16 by 16 cells.
All inputs are finite; a program needn't handle non-finite values.
Results may differ from a plain program's by a relative error of at most 0.0073.
Values may be sent and summed in bfloat16 or wider, within the bound.
No kernel may reach another device: no remote copies, remote signals or barrier semaphores. Data moves between devices by JAX's collectives and lax.ppermute only.
A program may use at most 128 MiB of HBM per device.

v0:
```python
import math
import jax
import jax.numpy as jnp
from jax import lax
from jax.sharding import PartitionSpec as P

THETA = 256.0


def rotate(tokens_in, positions):
    head_dim = tokens_in.shape[-1]
    band_t = head_dim // 8
    band_h = (head_dim - band_t) // 2
    band_w = head_dim - band_t - band_h
    values = tokens_in.astype(jnp.float32)
    pieces = []
    offset = 0
    for axis_index, band_size in ((0, band_t), (1, band_h), (2, band_w)):
        half_size = band_size // 2
        frequency = THETA ** (-2.0 * jnp.arange(half_size, dtype=jnp.float32) / band_size)
        angles = positions[axis_index].astype(jnp.float32)[:, None] * frequency[None, :]
        cos_table = jnp.cos(angles)[:, None, :]
        sin_table = jnp.sin(angles)[:, None, :]
        lower_half = values[:, :, offset : offset + half_size]
        upper_half = values[:, :, offset + half_size : offset + band_size]
        pieces.append(lower_half * cos_table - upper_half * sin_table)
        pieces.append(upper_half * cos_table + lower_half * sin_table)
        offset += band_size
    return jnp.concatenate(pieces, axis=-1).astype(jnp.bfloat16)


def local(video_q, video_k, video_v, positions, text_q, text_k, text_v, text_count):
    rotated_q = rotate(video_q, positions)
    rotated_k = rotate(video_k, positions)
    queries_video, keys_video, values_video = (
        lax.all_to_all(rotated_q, "hd", split_axis=1, concat_axis=0, tiled=True),
        lax.all_to_all(rotated_k, "hd", split_axis=1, concat_axis=0, tiled=True),
        lax.all_to_all(video_v, "hd", split_axis=1, concat_axis=0, tiled=True),
    )
    cycle_size = lax.axis_size("ctx")
    text_share = text_q.shape[0] // cycle_size
    own_text = lax.dynamic_slice_in_dim(text_q, lax.axis_index("ctx") * text_share, text_share, 0)
    queries = jnp.concatenate([queries_video, own_text], axis=0)
    scale = 1.0 / math.sqrt(queries.shape[-1])
    text_live = jnp.arange(text_k.shape[0], dtype=jnp.int32) < text_count[0]
    scores = jnp.einsum("qhd,khd->qhk", queries, text_k, preferred_element_type=jnp.float32) * scale
    scores = jnp.where(text_live[None, None, :], scores, -jnp.inf)
    peak = jnp.max(scores, axis=2)
    probs = jnp.exp(scores - peak[..., None])
    total = jnp.sum(probs, axis=2)
    mixed = jnp.einsum(
        "qhk,khd->qhd", probs.astype(jnp.bfloat16), text_v, preferred_element_type=jnp.float32
    )
    keys_all, values_all = (
        lax.all_gather(keys_video, "ctx", axis=0, tiled=True),
        lax.all_gather(values_video, "ctx", axis=0, tiled=True),
    )
    piece_scores = (
        jnp.einsum("qhd,khd->qhk", queries, keys_all, preferred_element_type=jnp.float32) * scale
    )
    new_peak = jnp.maximum(peak, jnp.max(piece_scores, axis=2))
    factor = jnp.exp(peak - new_peak)
    piece_probs = jnp.exp(piece_scores - new_peak[..., None])
    new_total = total * factor + jnp.sum(piece_probs, axis=2)
    new_mixed = mixed * factor[..., None] + jnp.einsum(
        "qhk,khd->qhd",
        piece_probs.astype(jnp.bfloat16),
        values_all,
        preferred_element_type=jnp.float32,
    )
    attended = (new_mixed / new_total[..., None]).astype(jnp.bfloat16)
    video_rows = queries_video.shape[0]
    video_heads = attended[:video_rows]
    text_out = attended[video_rows:]
    video_out = lax.all_to_all(video_heads, "hd", split_axis=0, concat_axis=1, tiled=True)
    return (video_out, text_out)


def solution(mesh):
    return jax.shard_map(
        local,
        mesh=mesh,
        in_specs=(
            P(("ctx", "hd"), "grp", None),
            P(("ctx", "hd"), "grp", None),
            P(("ctx", "hd"), "grp", None),
            P(None, ("ctx", "hd")),
            P(None, ("grp", "hd"), None),
            P(None, ("grp", "hd"), None),
            P(None, ("grp", "hd"), None),
            P(),
        ),
        out_specs=(P(("ctx", "hd"), "grp", None), P("ctx", ("grp", "hd"), None)),
        check_vma=False,
    )
```

profile of v0, /device:TPU:16, one launch (start us, length us, event | category | flops | bytes accessed | tf_op | source)
XLA Modules:
  0.0 811.1 jit_solution(17973969847977759047)
XLA Ops:
  7.2 0.0 copy-start
  7.2 0.0 all-gather.3.cloned.1.call-start
  7.3 0.8 convert_bitcast_fusion
  8.1 1.0 convert_element_type.50
  9.0 0.1 multiply_cosine_fusion.2
  9.1 0.1 copy.19
  9.2 0.1 copy.20
  9.3 1.0 convert_element_type.58
  10.3 0.3 multiply_cosine_fusion
  10.6 0.4 add_convert_fusion.5
  10.9 0.5 add_convert_fusion
  11.4 0.6 concatenate.13
  12.0 18.1 %all_to_all.72 = bf16[64,12,128]{2,0,1:T(8,128)(2,1)S(1)} all-to-all(bf16[64,12,128]{2,0,1:T(8,128)(2,1)S(1)} %concatenate.13), channel_id=1, replica_groups=mesh['grp'=2,'ctx'=64,'hd'=2] {'hd'}, dimensions={1} | all-to-all | bytes 393216 | tf_op jit(solution)/shard_map/all_to_all | solution.py:37
  30.1 0.7 copy.22
  30.8 0.0 all-gather.3.cloned.1.call-update
  30.8 0.0 all-gather.5.cloned.1.call-start
  30.9 12.4 %all_to_all.73 = bf16[64,12,128]{2,0,1:T(8,128)(2,1)S(1)} all-to-all(bf16[64,12,128]{2,0,1:T(8,128)(2,1)} %param.10), channel_id=1, replica_groups=mesh['grp'=2,'ctx'=64,'hd'=2] {'hd'}, dimensions={1} | all-to-all | bytes 393216 | tf_op jit(solution)/shard_map/all_to_all | solution.py:38
  43.3 0.7 copy.23
  44.0 0.0 all-gather.5.cloned.1.call-update
  44.0 0.5 add_convert_fusion.3
  44.5 1.2 concatenate.11
  45.7 3.4 all-to-all-start
  49.8 0.7 constant_dynamic-slice_fusion
  50.5 8.4 %all-to-all-done = bf16[64,12,128]{2,0,1:T(8,128)(2,1)S(1)} async-done(((bf16[64,12,128]{2,0,1:T(8,128)(2,1)}), bf16[64,12,128]{2,0,1:T(8,128)(2,1)S(1)}, u32[]{:S(2)}, u32[]{:S(2)}) %all-to-all-start) | async-done | bytes 196640 | tf_op jit(solution)/shard_map/all_to_all | solution.py:36
  58.9 0.0 copy-done
  58.9 0.5 fusion.24
  59.5 0.5 fusion.16
  59.9 338.1 %all-gather.3.cloned.1.call-done = bf16[8192,6,128]{2,0,1:T(8,128)(2,1)} async-done(((bf16[128,6,128]{2,0,1:T(8,128)(2,1)}), bf16[8192,6,128]{2,0,1:T(8,128)(2,1)}) %all-gather.3.cloned.1.call-update) | async-done | bytes 12582928 | tf_op jit(solution)/shard_map/all_gather | solution.py:55
  398.1 16.2 %bitcast_reduce_fusion = (f32[132,6]{0,1:T(8,128)S(1)}, f32[6,8192,132]{1,2,0:T(8,128)}) fusion(bf16[8192,6,128]{2,0,1:T(8,128)(2,1)} %all-gather.3.cloned.1.call-done, bf16[4,6,128]{2,0,1:T(4,128)(2,1)S(1)} %constant_dynamic-slice_fusion, bf16[128,6,128]{2,0,1:T(8,128)(2,1)S(1)} %bitcast.55), kind=kOutput, calls=%fused_computation.1 | convolution fusion | flops 1674325248 | bytes 38741088 | tf_op jit(solution)/shard_map/qhd,khd->qhk/dot_general | solution.py:59
  414.3 0.0 copy-start.1
  414.3 11.4 %fusion.1 = f32[132,6]{0,1:T(8,128)S(1)} fusion(f32[6,8192,132]{1,2,0:T(8,128)} %get-tuple-element.36, f32[132,6]{0,1:T(8,128)S(1)} %max.13), kind=kLoop, calls=%fused_computation.3 | loop fusion | flops 19463400 | bytes 25958592 | tf_op jit(solution)/shard_map/reduce_sum | solution.py:64
  425.8 348.9 %all-gather.5.cloned.1.call-done = bf16[8192,6,128]{2,0,1:T(8,128)(2,1)} async-done(((bf16[128,6,128]{2,0,1:T(8,128)(2,1)}), bf16[8192,6,128]{2,0,1:T(8,128)(2,1)}) %all-gather.5.cloned.1.call-update) | async-done | bytes 12582928 | tf_op jit(solution)/shard_map/all_gather | solution.py:56
  774.6 15.2 %fusion.12 = f32[132,6,128]{2,0,1:T(8,128)S(1)} fusion(bf16[8192,6,128]{2,0,1:T(8,128)(2,1)} %all-gather.5.cloned.1.call-done, f32[6,8192,132]{1,2,0:T(8,128)} %get-tuple-element.36, f32[132,6]{0,1:T(8,128)S(1)} %max.13), kind=kOutput, calls=%fused_computation.15 | convolution fusion | flops 1680408576 | bytes 38943840 | tf_op jit(solution)/shard_map/qhk,khd->qhd/dot_general | solution.py:65
  789.8 0.0 copy-done.1
  789.8 0.4 fusion.15
  790.2 0.8 copy.24
  791.1 3.4 all-to-all-start.3
  794.5 0.6 slice.84
  795.1 8.5 %all-to-all-done.3 = bf16[128,6,128]{2,1,0:T(8,128)(2,1)S(1)} async-done(((bf16[128,6,128]{2,1,0:T(8,128)(2,1)}), bf16[128,6,128]{2,1,0:T(8,128)(2,1)S(1)}, u32[]{:S(2)}, u32[]{:S(2)}) %all-to-all-start.3) | async-done | bytes 196640 | tf_op jit(solution)/shard_map/all_to_all | solution.py:75
  803.6 0.7 copy.25
  (7 shorter events, 0.1 us)
Async XLA Ops:
  7.2 51.8 %copy-start = (bf16[256,6,128]{2,0,1:T(8,128)(2,1)S(1)}, bf16[256,6,128]{2,0,1:T(8,128)(2,1)}, u32[]{:S(2)}) copy-start(bf16[256,6,128]{2,0,1:T(8,128)(2,1)} %param.13) | copy-start | bytes 1179652
  7.2 390.9 %all-gather.3.cloned.1.call-start = ((), (), s32[]{:S(2)}) async-start(), calls=%async_computation.4 | async-start | bytes 12779520 | tf_op jit(solution)/shard_map/all_gather | solution.py:55
  30.8 743.8 %all-gather.5.cloned.1.call-start = ((), (), s32[]{:S(2)}) async-start(), calls=%async_computation.5 | async-start | bytes 12779520 | tf_op jit(solution)/shard_map/all_gather | solution.py:56
  45.7 13.2 %all-to-all-start = ((bf16[64,12,128]{2,0,1:T(8,128)(2,1)}), bf16[64,12,128]{2,0,1:T(8,128)(2,1)S(1)}, u32[]{:S(2)}, u32[]{:S(2)}) async-start(bf16[64,12,128]{2,0,1:T(8,128)(2,1)} %concatenate.11), calls=%async_computation | async-start | bytes 393216 | tf_op jit(solution)/shard_map/all_to_all | solution.py:36
  414.3 375.5 %copy-start.1 = (bf16[256,6,128]{2,0,1:T(8,128)(2,1)S(1)}, bf16[256,6,128]{2,0,1:T(8,128)(2,1)}, u32[]{:S(2)}) copy-start(bf16[256,6,128]{2,0,1:T(8,128)(2,1)} %param.14) | copy-start | bytes 1179652
  791.1 12.5 %all-to-all-start.3 = ((bf16[128,6,128]{2,1,0:T(8,128)(2,1)}), bf16[128,6,128]{2,1,0:T(8,128)(2,1)S(1)}, u32[]{:S(2)}, u32[]{:S(2)}) async-start(bf16[128,6,128]{2,1,0:T(8,128)(2,1)} %copy.24), calls=%async_computation.3 | async-start | bytes 524288 | tf_op jit(solution)/shard_map/all_to_all | solution.py:75
Sparse Core Ops, SparseCore 0:
  31.0 367.0 all-gather.2
  400.4 374.1 all-gather.4
where the time goes:
time: 812 us; the launch traced here: 811 us
  waiting for transfers between devices  704 us (87%)
  matrix products  32.4 us (4%)
  blocking collectives  30.5 us (4%)
  other arithmetic  16.3 us (2%)
  between operations  14.8 us (2%)
    all_gather x1, waiting for transfers between devices, local(): lax.all_gather(values_video, 'ctx', axis=0, tiled=True)  349 us
    all_gather x1, waiting for transfers between devices, local(): lax.all_gather(keys_video, 'ctx', axis=0, tiled=True)  338 us
    all_to_all x1, blocking collectives, local(): lax.all_to_all(rotated_k, 'hd', split_axis=1, concat_axis=0, tiled=True)  18.1 us
    dot_general x1, matrix products, local(): jnp.einsum('qhd,khd->qhk', queries, keys_all, preferred_element_type=jnp....  16.2 us
  transfers between devices with their start and end apart: 4, of which 4 were waited for; matrix products, arithmetic and copies ran while one was open for 4% of the time, Pallas kernels for 0%

commit v1 on v0

--- a/solution.py
+++ b/solution.py
@@ -3,6 +3,7 @@
 import jax.numpy as jnp
 from jax import lax
 from jax.sharding import PartitionSpec as P
+from jax.lax import all_to_all, axis_size
 
 THETA = 256.0
 
@@ -51,9 +52,18 @@
     mixed = jnp.einsum(
         "qhk,khd->qhd", probs.astype(jnp.bfloat16), text_v, preferred_element_type=jnp.float32
     )
+    produce_pages = lambda content: jnp.concatenate(
+        all_to_all(
+            jnp.stack([content for _ in range(axis_size("ctx"))], axis=0),
+            axis_name="ctx",
+            split_axis=0,
+            concat_axis=0,
+        ),
+        axis=0,
+    )
     keys_all, values_all = (
         lax.all_gather(keys_video, "ctx", axis=0, tiled=True),
-        lax.all_gather(values_video, "ctx", axis=0, tiled=True),
+        produce_pages(values_video),
     )
     piece_scores = (
         jnp.einsum("qhd,khd->qhk", queries, keys_all, preferred_element_type=jnp.float32) * scale

time: 812 us -> 592 us (0.73)
  waiting for transfers between devices: 704 us -> 458 us
  local copies, waits for them, and re-layouts: 6.24 us -> 24.1 us
  starting transfers between devices: 6.95 us -> 22.2 us
  blocking collectives: 30.5 us -> 18.1 us
    all_gather x1 -> x0, waiting for transfers between devices: 349 us -> none  [local(): lax.all_gather(values_video, 'ctx', axis=0, tiled=True)]
    all_gather x1, waiting for transfers between devices: 338 us -> 433 us  [local(): lax.all_gather(keys_video, 'ctx', axis=0, tiled=True)]
    all_to_all x0 -> x2, starting transfers between devices: none -> 14.9 us  [the longest x1 11.5 us: local(): all_to_all(jnp.stack([content for _ in range(axis_size('ctx'))], axis=0),...]
    all_to_all x1 -> x0, blocking collectives: 12.4 us -> none  [local(): lax.all_to_all(video_v, 'hd', split_axis=1, concat_axis=0, tiled=True)]
    all_to_all x0 -> x1, local copies, waits for them, and re-layouts: none -> 10.8 us  [local(): all_to_all(jnp.stack([content for _ in range(axis_size('ctx'))], axis=0),...]
  transfers between devices with their start and end apart: 4 -> 5, of which waited for: 4 -> 4; matrix products, arithmetic and copies ran while one was open for 4% -> 7% of each run, Pallas kernels for 0% -> 0%
where the time goes in v1:
time: 592 us; the launch traced here: 586 us
  waiting for transfers between devices  458 us (77%)
  matrix products  32.3 us (5%)
  local copies, waits for them, and re-layouts  24.1 us (4%)
  starting transfers between devices  22.2 us (4%)
  blocking collectives  18.1 us (3%)
  other arithmetic  16.2 us (3%)
  between operations  14.9 us (3%)
    all_gather x1, waiting for transfers between devices, local(): lax.all_gather(keys_video, 'ctx', axis=0, tiled=True)  433 us
    all_to_all x1, blocking collectives, local(): lax.all_to_all(rotated_k, 'hd', split_axis=1, concat_axis=0, tiled=True)  18.1 us
    dot_general x1, matrix products, local(): jnp.einsum('qhd,khd->qhk', queries, keys_all, preferred_element_type=jnp....  16.2 us
    dot_general x1, matrix products, local(): jnp.einsum('qhk,khd->qhd', piece_probs.astype(jnp.bfloat16), values_all,...  15.2 us
  transfers between devices with their start and end apart: 5, of which 4 were waited for; matrix products, arithmetic and copies ran while one was open for 7% of the time, Pallas kernels for 0%

profile of v1, /device:TPU:16, one launch (start us, length us, event | category | flops | bytes accessed | tf_op | source)
XLA Modules:
  0.0 586.1 jit_solution(16272584318323827168)
XLA Ops:
  7.2 0.0 copy-start
  7.2 0.0 all-gather.2.cloned.1.call-start
  7.3 1.0 convert_element_type.50
  8.3 0.8 convert_bitcast_fusion
  9.1 0.1 multiply_cosine_fusion.2
  9.2 0.1 copy.27
  9.2 0.1 copy.26
  9.3 1.0 convert_element_type.58
  10.3 0.3 multiply_cosine_fusion
  10.6 0.4 add_convert_fusion.5
  11.0 0.5 add_convert_fusion
  11.5 0.6 concatenate.13
  12.1 18.1 %all_to_all.74 = bf16[64,12,128]{2,0,1:T(8,128)(2,1)S(1)} all-to-all(bf16[64,12,128]{2,0,1:T(8,128)(2,1)S(1)} %concatenate.13), channel_id=1, replica_groups=mesh['grp'=2,'ctx'=64,'hd'=2] {'hd'}, dimensions={1} | all-to-all | bytes 393216 | tf_op jit(solution)/shard_map/all_to_all | solution.py:38
  30.2 0.7 copy.29
  30.8 0.0 all-gather.2.cloned.1.call-update
  30.9 3.4 all-to-all-start.2
  34.3 0.5 add_convert_fusion.3
  34.8 1.2 concatenate.11
  36.0 7.3 %all-to-all-done.2 = bf16[64,12,128]{2,0,1:T(8,128)(2,1)S(1)} async-done(((bf16[64,12,128]{2,0,1:T(8,128)(2,1)}), bf16[64,12,128]{2,0,1:T(8,128)(2,1)S(1)}, u32[]{:S(2)}, u32[]{:S(2)}) %all-to-all-start.2) | async-done | bytes 196640 | tf_op jit(solution)/shard_map/all_to_all | solution.py:39
  43.3 3.4 all-to-all-start
  46.8 9.8 %all-to-all-done = bf16[64,12,128]{2,0,1:T(8,128)(2,1)S(1)} async-done(((bf16[64,12,128]{2,0,1:T(8,128)(2,1)}), bf16[64,12,128]{2,0,1:T(8,128)(2,1)S(1)}, u32[]{:S(2)}, u32[]{:S(2)}) %all-to-all-start) | async-done | bytes 196640 | tf_op jit(solution)/shard_map/all_to_all | solution.py:37
  56.5 7.8 %stack.5 = bf16[64,128,6,128]{3,1,2,0:T(8,128)(2,1)} broadcast(bf16[128,6,128]{2,0,1:T(8,128)(2,1)S(1)} %bitcast.63), dimensions={1,2,3} | broadcast | bytes 12779520 | tf_op jit(solution)/shard_map/stack | solution.py:57
  64.3 11.5 %all-to-all-start.3 = ((bf16[64,128,6,128]{3,1,2,0:T(8,128)(2,1)}), bf16[64,128,6,128]{3,1,2,0:T(8,128)(2,1)}, u32[]{:S(2)}, u32[]{:S(2)}) async-start(bf16[64,128,6,128]{3,1,2,0:T(8,128)(2,1)} %stack.5), calls=%async_computation.3 | async-start | bytes 25165824 | tf_op jit(solution)/shard_map/all_to_all | solution.py:56
  76.4 0.7 constant_dynamic-slice_fusion
  77.2 0.0 copy-done
  77.2 0.5 fusion.24
  77.7 0.5 fusion.16
  78.2 432.6 %all-gather.2.cloned.1.call-done = bf16[8192,6,128]{2,0,1:T(8,128)(2,1)} async-done(((bf16[128,6,128]{2,0,1:T(8,128)(2,1)}), bf16[8192,6,128]{2,0,1:T(8,128)(2,1)}) %all-gather.2.cloned.1.call-update) | async-done | bytes 12582928 | tf_op jit(solution)/shard_map/all_gather | solution.py:65
  510.8 16.2 %bitcast_reduce_fusion = (f32[132,6]{0,1:T(8,128)S(1)}, f32[6,8192,132]{1,2,0:T(8,128)}) fusion(bf16[8192,6,128]{2,0,1:T(8,128)(2,1)} %all-gather.2.cloned.1.call-done, bf16[4,6,128]{2,0,1:T(4,128)(2,1)S(1)} %constant_dynamic-slice_fusion, bf16[128,6,128]{2,0,1:T(8,128)(2,1)S(1)} %bitcast.57), kind=kOutput, calls=%fused_computation.1 | convolution fusion | flops 1674325248 | bytes 38741088 | tf_op jit(solution)/shard_map/qhd,khd->qhk/dot_general | solution.py:69
  527.0 11.3 %fusion.1 = f32[132,6]{0,1:T(8,128)S(1)} fusion(f32[6,8192,132]{1,2,0:T(8,128)} %get-tuple-element.36, f32[132,6]{0,1:T(8,128)S(1)} %max.13), kind=kLoop, calls=%fused_computation.3 | loop fusion | flops 19463400 | bytes 25958592 | tf_op jit(solution)/shard_map/reduce_sum | solution.py:74
  538.3 0.0 copy-start.2
  538.3 0.0 all-to-all-done.3
  538.3 0.0 copy-start.1
  538.4 10.8 %copy.31 = bf16[64,128,6,128]{3,1,0,2:T(8,128)(2,1)} copy(bf16[64,128,6,128]{3,1,2,0:T(8,128)(2,1)} %all-to-all-done.3) | data formatting | bytes 25165824 | tf_op jit(solution)/shard_map/all_to_all | solution.py:56
  549.1 15.2 %fusion.12 = f32[132,6,128]{2,0,1:T(8,128)S(1)} fusion(bf16[8192,6,128]{2,0,1:T(8,128)(2,1)} %bitcast.55, f32[6,8192,132]{1,2,0:T(8,128)} %get-tuple-element.36, f32[132,6]{0,1:T(8,128)S(1)} %max.13), kind=kOutput, calls=%fused_computation.15 | convolution fusion | flops 1680408576 | bytes 38943840 | tf_op jit(solution)/shard_map/qhk,khd->qhd/dot_general | solution.py:75
  564.3 0.0 copy-done.2
  564.3 0.4 fusion.15
  564.8 0.8 copy.32
  565.6 3.8 all-to-all-start.4
  569.4 0.6 slice.84
  570.0 8.5 %all-to-all-done.4 = bf16[128,6,128]{2,1,0:T(8,128)(2,1)S(1)} async-done(((bf16[128,6,128]{2,1,0:T(8,128)(2,1)}), bf16[128,6,128]{2,1,0:T(8,128)(2,1)S(1)}, u32[]{:S(2)}, u32[]{:S(2)}) %all-to-all-start.4) | async-done | bytes 196640 | tf_op jit(solution)/shard_map/all_to_all | solution.py:85
  578.5 0.7 copy.33
  579.2 0.0 copy-done.1
  (8 shorter events, 0.1 us)
Async XLA Ops:
  7.2 70.0 %copy-start = (bf16[256,6,128]{2,0,1:T(8,128)(2,1)S(1)}, bf16[256,6,128]{2,0,1:T(8,128)(2,1)}, u32[]{:S(2)}) copy-start(bf16[256,6,128]{2,0,1:T(8,128)(2,1)} %param.13) | copy-start | bytes 1179652
  7.2 503.6 %all-gather.2.cloned.1.call-start = ((), (), s32[]{:S(2)}) async-start(), calls=%async_computation.5 | async-start | bytes 12779520 | tf_op jit(solution)/shard_map/all_gather | solution.py:65
  30.9 12.4 %all-to-all-start.2 = ((bf16[64,12,128]{2,0,1:T(8,128)(2,1)}), bf16[64,12,128]{2,0,1:T(8,128)(2,1)S(1)}, u32[]{:S(2)}, u32[]{:S(2)}) async-start(bf16[64,12,128]{2,0,1:T(8,128)(2,1)} %param.10), calls=%async_computation.2 | async-start | bytes 393216 | tf_op jit(solution)/shard_map/all_to_all | solution.py:39
  43.3 13.2 %all-to-all-start = ((bf16[64,12,128]{2,0,1:T(8,128)(2,1)}), bf16[64,12,128]{2,0,1:T(8,128)(2,1)S(1)}, u32[]{:S(2)}, u32[]{:S(2)}) async-start(bf16[64,12,128]{2,0,1:T(8,128)(2,1)} %concatenate.11), calls=%async_computation | async-start | bytes 393216 | tf_op jit(solution)/shard_map/all_to_all | solution.py:37
  64.3 474.1 %all-to-all-start.3 = ((bf16[64,128,6,128]{3,1,2,0:T(8,128)(2,1)}), bf16[64,128,6,128]{3,1,2,0:T(8,128)(2,1)}, u32[]{:S(2)}, u32[]{:S(2)}) async-start(bf16[64,128,6,128]{3,1,2,0:T(8,128)(2,1)} %stack.5), calls=%async_computation.3 | async-start | bytes 25165824 | tf_op jit(solution)/shard_map/all_to_all | solution.py:56
  538.3 26.0 %copy-start.2 = (bf16[256,6,128]{2,0,1:T(8,128)(2,1)S(1)}, bf16[256,6,128]{2,0,1:T(8,128)(2,1)}, u32[]{:S(2)}) copy-start(bf16[256,6,128]{2,0,1:T(8,128)(2,1)} %param.14) | copy-start | bytes 1179652
  538.3 40.9 %copy-start.1 = (bf16[256,6,128]{2,0,1:T(8,128)(2,1)S(1)}, bf16[256,6,128]{2,0,1:T(8,128)(2,1)}, u32[]{:S(2)}) copy-start(bf16[256,6,128]{2,0,1:T(8,128)(2,1)} %param.13) | copy-start | bytes 1179652
  565.6 12.9 %all-to-all-start.4 = ((bf16[128,6,128]{2,1,0:T(8,128)(2,1)}), bf16[128,6,128]{2,1,0:T(8,128)(2,1)S(1)}, u32[]{:S(2)}, u32[]{:S(2)}) async-start(bf16[128,6,128]{2,1,0:T(8,128)(2,1)} %copy.32), calls=%async_computation.4 | async-start | bytes 524288 | tf_op jit(solution)/shard_map/all_to_all | solution.py:85
Sparse Core Ops, SparseCore 0:
  31.0 479.7 all-gather.1
